TPU v7x, 32 devices: a whole 2x2x4 slice. The times are simulated.
32 devices in a mesh: dp: 16 (over z, x, core), spk: 2 (over y).
Axes of the slice: x: 2, y: 2, z: 4, core: 2. Of those that a mesh axis runs over, the one named last changes fastest.
Arguments:
- spans: bfloat16 [512, 100, 64], P(('dp', 'spk')), may hold values from -6 to 6
- encoded: bfloat16 [25600, 64], P(('dp', 'spk')), may hold values from -6 to 6
- clip_lengths: int32 [16, 2, 3], P('dp'), may hold values from 1 to 12, 16 in all within a row
- clip_pads: int32 [16, 2, 3], P('dp'), may hold values from 0 to 49
- lstm_in: bfloat16 [2, 2, 2, 64, 512], replicated, may hold values from -0.75 to 0.75
- lstm_rec: bfloat16 [2, 2, 2, 128, 512], replicated, may hold values from -0.5 to 0.5
- lstm_bias: float32 [2, 2, 2, 512], replicated, may hold values from -3 to 3
- proj_weight: bfloat16 [2, 2, 256, 64], replicated, may hold values from -0.375 to 0.375
- proj_bias: float32 [2, 2, 64], replicated, may hold values from -3 to 3
- gln_gain: float32 [2, 2, 64], replicated, may hold values from 0.25 to 1.75
- gln_shift: float32 [2, 2, 64], replicated, may hold values from -3 to 3
- mask_weight: bfloat16 [2, 64, 64], P('spk'), may hold values from -0.75 to 0.75
- mask_bias: bfloat16 [2, 64], P('spk'), may hold values from -3 to 3
- dec_weight: bfloat16 [64, 16], replicated, may hold values from -0.75 to 0.75
- wave_grad: bfloat16 [2, 204800], P('spk', 'dp'), may hold values from -6 to 6
Outputs:
- waveforms: float32 [2, 204800], P('spk', 'dp')
- grad_spans: float32 [512, 100, 64], P(('dp', 'spk'))
- grad_lstm_in: float32 [2, 2, 2, 64, 512], replicated
- grad_lstm_rec: float32 [2, 2, 2, 128, 512], replicated
- grad_lstm_bias: float32 [2, 2, 2, 512], replicated
- grad_proj_weight: float32 [2, 2, 256, 64], replicated
- grad_proj_bias: float32 [2, 2, 64], replicated
- grad_gln_gain: float32 [2, 2, 64], replicated
- grad_gln_shift: float32 [2, 2, 64], replicated
- grad_mask_weight: float32 [2, 64, 64], P('spk')
- grad_mask_bias: float32 [2, 64], P('spk')
- grad_dec_weight: float32 [64, 16], replicated
Inputs may be any that keep to these rules, and one draw needn't show every extreme that they name: `clip_lengths`: each device's 3 counts sum to 16, and on every device the longest is exactly 12.
All inputs are finite; a program needn't handle non-finite values.
Results may differ from a plain program's by a relative error of at most 0.013.
Values may be sent and summed in bfloat16 or wider, within the bound.
A program may use at most 192 MiB of HBM per device.

v0:
```python
import functools

import jax
import jax.numpy as jnp
from jax import lax
from jax.experimental import pallas as pl
from jax.experimental.pallas import tpu as pltpu
from jax.sharding import PartitionSpec as P

F32 = jnp.float32
BF16 = jnp.bfloat16
LANES = 128
PART = 16
PAIR = 2 * PART
MESH = pl.DeviceIdType.MESH


def dot(a, b):
    return jnp.dot(a, b, preferred_element_type=F32)


def dot_tn(a, b):
    return lax.dot_general(a, b, (((0,), (0,)), ((), ())), preferred_element_type=F32)


def dot_nt(a, b):
    return lax.dot_general(a, b, (((1,), (1,)), ((), ())), preferred_element_type=F32)


def chunks(total, size, body):
    assert total % size == 0

    def step(i, carry):
        body(pl.multiple_of(i * size, size))
        return carry

    lax.fori_loop(0, total // size, step, 0)


class Place:
    def __init__(self, num_dp):
        self.dp, self.spk = lax.axis_index("dp"), lax.axis_index("spk")
        self.bits = num_dp.bit_length()

    def bit(self, k):
        if k == 1:
            return self.spk
        return self.dp // (1 << max(k - 1, 0)) % 2

    def device(self, mask):
        dp, spk = self.dp, self.spk
        for k in range(self.bits):
            if mask >> k & 1:
                if k == 1:
                    spk = 1 - spk
                else:
                    dp = dp + (1 - 2 * self.bit(k)) * (1 << max(k - 1, 0))
        return {"dp": dp, "spk": spk}

    def index(self, bits, mask=0):
        number = 0
        for i, k in enumerate(bits):
            one = 1 - self.bit(k) if mask >> k & 1 else self.bit(k)
            number = number + one * (1 << i)
        return number

    def masks(self, bits):
        found = []
        for m in range((1 << len(bits)) - 1, 0, -1):
            found.append(sum((m >> i & 1) << k for i, k in enumerate(bits)))
        return found


class Reduction:
    def __init__(self, buf, recv, out, sems, place, stages, outer, times):
        self.buf, self.recv, self.out, self.sems, self.place = buf, recv, out, sems, place
        self.steps, back = [], []
        off, size, at, sem = 0, buf.shape[0], 0, 0
        for i, bits in enumerate(stages):
            masks = place.masks(bits)
            part = size // (len(masks) + 1)
            own = off + place.index(bits) * part
            last = i == len(stages) - 1
            self.steps.append(
                (
                    functools.partial(self.scatter, sem, masks, bits, off, part, at),
                    functools.partial(self.add, len(masks), own, part, at, out if last else buf),
                    times[len(bits)],
                )
            )
            back.append((masks, own, part, times[len(bits)]))
            off, size = own, part
            at += len(masks) * part
            sem += 1
        for k in outer:
            self.steps.append(
                (
                    functools.partial(self.double, sem, k, off, size, at),
                    functools.partial(self.add_double, off, size, at),
                    times[1],
                )
            )
            at += size
            sem += 1
        for masks, own, part, time in reversed(back):
            self.steps.append((functools.partial(self.gather, sem, masks, own, part), None, time))
            sem += 1
        self.pending, self.after, self.due = None, None, 0.0

    def copy(self, sem, src, dst, device):
        return pltpu.make_async_remote_copy(
            src_ref=src,
            dst_ref=dst,
            send_sem=self.sems.at[sem, 0],
            recv_sem=self.sems.at[sem, 1],
            device_id=device,
            device_id_type=MESH,
        )

    def rows(self, ref, off, size):
        return ref.at[pl.ds(pl.multiple_of(off, PART), size)]

    def all_of(self, sem, masks, part):
        rows = self.recv.at[0 : len(masks) * part]
        return self.copy(sem, rows, rows, self.place.device(masks[0]))

    def scatter(self, sem, masks, bits, off, part, at):
        for i, mask in enumerate(masks):
            src = self.rows(self.buf, off + self.place.index(bits, mask) * part, part)
            dst = self.recv.at[at + i * part : at + (i + 1) * part]
            self.copy(sem, src, dst, self.place.device(mask)).start()
        return self.all_of(sem, masks, part)

    def add(self, number, own, part, at, target):
        def body(i, carry):
            rows = pl.ds(pl.multiple_of(own + i * PART, PART), PART)
            for lanes in [slice(x, x + LANES) for x in range(0, self.buf.shape[1], LANES)]:
                total = self.buf[rows, lanes].astype(F32)
                for q in range(number):
                    new = pl.ds(pl.multiple_of(at + q * part + i * PART, PART), PART)
                    total = total + self.recv[new, lanes].astype(F32)
                target[rows, lanes] = total.astype(BF16)
            return carry

        lax.fori_loop(0, part // PART, body, 0)

    def double(self, sem, k, off, size, at):
        copy = self.copy(sem, self.rows(self.out, off, size), self.recv.at[at : at + size], self.place.device(1 << k))
        copy.start()
        return copy

    def add_double(self, off, size, at):
        rows = pl.ds(pl.multiple_of(off, PART), size)
        self.out[rows] = (self.out[rows].astype(F32) + self.recv[at : at + size].astype(F32)).astype(BF16)

    def gather(self, sem, masks, own, part):
        rows = self.rows(self.out, own, part)
        for mask in masks:
            self.copy(sem, rows, rows, self.place.device(mask)).start()
        return self.all_of(sem, masks, part)

    def advance(self, now):
        if self.pending is not None:
            self.pending.wait()
            if self.after is not None:
                self.after()
            self.pending = None
        if self.steps:
            start, self.after, time = self.steps.pop(0)
            self.pending = start()
            self.due = now + time

    def over(self):
        return self.pending is None and not self.steps


def local_kernel(
    sizes,
    lengths_ref,
    pads_ref,
    spans_ref,
    enc_ref,
    w_in_ref,
    w_rec_ref,
    w_bias_ref,
    w_proj_ref,
    proj_bias_ref,
    gain_ref,
    shift_ref,
    mask_in_ref,
    mask_bias_in_ref,
    dec_in_ref,
    wave_grad_ref,
    wave_out,
    spans_out,
    sums_out,
    stream,
    valid,
    mx,
    xj,
    dz,
    dmj,
    normed,
    inv_all,
    u_a,
    u_e,
    hc_a,
    hc_e,
    sv_a,
    sv_e,
    gd,
    dh,
    dp,
    wcat,
    wit,
    wrt,
    pws,
    vec,
    enc_t,
    pre,
    masked,
    feats,
    dpre,
    mask_ref,
    dec_ref,
    send,
    own,
    got,
    wave_got,
    sems,
    sums,
    recv,
    small,
    sum_sems,
    all_sums,
    grad_spans,
    out_sems,
):
    R, K, C, H, clips, blocks, kp, num_dp = sizes
    rows, rows_e = R * K, R * kp
    hop = K // 2
    frames = R * hop
    half = dec_in_ref.shape[0] // 2
    wr = frames * half // LANES
    group = LANES // half
    cr = rows
    speaker = lax.axis_index("spk")
    partner = {"spk": 1 - speaker}

    barrier = pltpu.get_barrier_semaphore()
    place = Place(num_dp)
    everyone = place.masks(range(1, min(place.bits, 5))) + [1 << k for k in [0, *range(5, place.bits)]]
    for mask in everyone:
        pl.semaphore_signal(barrier, inc=1, device_id=place.device(mask), device_id_type=MESH)

    mask_row = -(-wr // 8) * 8
    for i in range(wr):
        at = pl.multiple_of(speaker * (wr * LANES) + i * LANES, LANES)
        own[i : i + 1] = wave_grad_ref[0:1, pl.ds(at, LANES)].astype(F32)
        at = pl.multiple_of((1 - speaker) * (wr * LANES) + i * LANES, LANES)
        send[i : i + 1] = wave_grad_ref[0:1, pl.ds(at, LANES)].astype(F32)
    mask_f = mask_in_ref[0].astype(F32)
    send[wr:mask_row] = jnp.zeros((mask_row - wr, LANES), F32)
    send[mask_row : mask_row + C] = jnp.concatenate([mask_f, mask_f], axis=1)
    bias_f = mask_bias_in_ref[0:1].astype(F32)
    bias_f = jnp.concatenate([bias_f, bias_f], axis=1)
    send[mask_row + C : mask_row + C + 8] = jnp.broadcast_to(bias_f, (8, LANES))

    jio = lax.broadcasted_iota(jnp.int32, (R, LANES), 0)
    lane = lax.broadcasted_iota(jnp.int32, (1, LANES), 1)
    ones_lanes = jnp.logical_and(lane >= C, lane < C + 3)

    lens = [lengths_ref[0, speaker, c] for c in range(clips)]
    pads = [pads_ref[0, speaker, c] for c in range(clips)]
    starts, ends, at = [], [], 0
    for c in range(clips):
        starts.append(at)
        at = at + lens[c]
        ends.append(at)

    def is_start(j):
        hit = j == starts[0]
        for c in range(1, clips):
            hit = jnp.logical_or(hit, j == starts[c])
        return hit

    def is_end(j):
        hit = j == ends[0] - 1
        for c in range(1, clips):
            hit = jnp.logical_or(hit, j == ends[c] - 1)
        return hit

    members, thr, inv_count = [], jnp.full((R, LANES), K, jnp.int32), jnp.zeros((R, LANES), F32)
    for c in range(clips):
        member = jnp.logical_and(jio >= starts[c], jio < ends[c]).astype(F32)
        members.append(member)
        thr = jnp.where(jio == ends[c] - 1, K - pads[c], thr)
        count = (C * (K * lens[c] - pads[c])).astype(F32)
        inv_count = inv_count + member / jnp.full((R, LANES), count, F32)
    not_first = 1.0 - is_start(jio).astype(F32)
    next_not_first = 1.0 - jnp.logical_or(is_start(jio + 1), jio == R - 1).astype(F32)

    def clip_sum(x):
        out = jnp.zeros((R, 1), F32)
        for member in members:
            out = out + member[:, :1] * jnp.sum(member * x, axis=(0, 1), keepdims=True)
        return out

    def fill_valid(r):
        k = lax.broadcasted_iota(jnp.int32, (cr // R, R, LANES), 0) + r // R
        low = lax.broadcasted_iota(jnp.int32, (cr // R, R, LANES), 2) < C
        ok = jnp.logical_and(k < thr[None], low).astype(F32)
        valid[pl.ds(r, cr)] = ok.reshape(cr, LANES)

    chunks(rows, cr, fill_valid)

    near, far = list(range(1, min(place.bits, 3))), list(range(3, min(place.bits, 5)))
    outer = range(5, place.bits)
    times = {1: 1.7, 2: 4.2, 4: 6.8}

    def reduction(n, stages):
        reduce = Reduction(sums.at[n], recv.at[n], all_sums.at[n], sum_sems.at[n], place, stages, outer, times)
        reduce.number = n
        return reduce

    lay = sum_rows(C, H)
    active = []
    clock = [0.0]

    def point(passed):
        clock[0] += passed
        for reduce in active:
            if not reduce.over() and reduce.due <= clock[0]:
                reduce.advance(clock[0])

    for n in range(2 * blocks):
        for at in (lay["proj"], lay["head"]):
            sums[n, at : at + PAIR] = jnp.zeros((PAIR, 4 * H), BF16)

    pws[...] = jnp.zeros_like(pws)
    wit[...] = jnp.zeros_like(wit)
    vec[...] = jnp.zeros_like(vec)
    for b in range(blocks):
        for s in range(2):
            n = 2 * b + s
            pws[b, s, 0:C] = w_proj_ref[b, s]
            vec[n, 0:1, 0:C] = proj_bias_ref[b, s : s + 1]
            vec[n, 1:2, 0:C] = gain_ref[b, s : s + 1]
            vec[n, 2:3, 0:C] = shift_ref[b, s : s + 1]

    stream[...] = jnp.zeros_like(stream)
    for j in range(R):
        x = spans_ref[j].astype(F32)
        x = jnp.concatenate([x, jnp.zeros_like(x)], axis=0).T
        stream[pl.ds(j, K, stride=R), :] = x

    def start_stream(r):
        x = stream[pl.ds(r, cr)] * valid[pl.ds(r, cr)]
        stream[pl.ds(r, cr)] = jnp.where(ones_lanes, 1.0, x)

    chunks(rows, cr, start_stream)

    gate_scale = jnp.where(
        lax.broadcasted_iota(jnp.int32, (1, 4 * H), 1) // H == 2, 1.0, 0.5
    ).astype(F32)

    def lane_part(x, g):
        return x[:, g * H : (g + 1) * H]

    def gate_step(d, sv, b, r, n, p, c, keep_next):
        acts = [jnp.tanh(p[:, g * H : (g + 1) * H]) for g in range(4)]
        ti, tf, g, to = acts
        i, f, o = 0.5 * ti + 0.5, 0.5 * tf + 0.5, 0.5 * to + 0.5
        cn = f * c + i * g
        tc = jnp.tanh(cn)
        h = o * tc
        parts = [
            g * (0.25 - 0.25 * ti * ti),
            c * (0.25 - 0.25 * tf * tf),
            i * (1.0 - g * g),
            tc * (0.25 - 0.25 * to * to),
            o * (1.0 - tc * tc),
            f,
        ]
        for m, part in enumerate(parts):
            sv[b, d, pl.ds(r, n), m * H : (m + 1) * H] = part.astype(BF16)
        if keep_next is None:
            return h.astype(BF16), h.astype(BF16), cn
        return h.astype(BF16), (h * keep_next).astype(BF16), cn * keep_next

    def run_forward(b, sec, u, hc, sv, n, steps, unroll):
        total = n * steps
        for d in range(2):
            wcat[d, 0:H] = (w_rec_ref[b, sec, d].astype(F32) * gate_scale).astype(BF16)
            wcat[d, H : H + C] = (w_in_ref[b, sec, d].astype(F32) * gate_scale).astype(BF16)
            bias = w_bias_ref[b, sec, d : d + 1] * gate_scale
            terms = []
            for _ in range(3):
                terms.append(bias.astype(BF16).astype(F32))
                bias = bias - terms[-1]
            row = lax.broadcasted_iota(jnp.int32, (H - C, 4 * H), 0)
            block = jnp.zeros((H - C, 4 * H), F32)
            for m, term in enumerate(terms):
                block = jnp.where(row == m, jnp.broadcast_to(term, block.shape), block)
            wcat[d, H + C : 2 * H] = block.astype(BF16)

        def step(t, carry):
            hf, hb, cf, cb = carry
            back = steps - 1 - t
            rf, rb = t * n, back * n
            if sec == 0:
                rf, rb = pl.multiple_of(rf, n), pl.multiple_of(rb, n)
            kf = kb = None
            if sec == 1:
                kf = 1.0 - is_start(t + 1).astype(F32)
                kb = 1.0 - is_end(back - 1).astype(F32)
            if sec == 1 and t < steps // 2:
                uf = stream[pl.ds(t, n, stride=R), :].astype(BF16)
                ub = stream[pl.ds(back, n, stride=R), :].astype(BF16)
                u[b, rf : rf + n] = uf
                u[b, rb : rb + n] = ub
            else:
                uf, ub = u[b, pl.ds(rf, n)], u[b, pl.ds(rb, n)]
            pf = dot(jnp.concatenate([hf, uf], axis=1), wcat[0])
            pb = dot(jnp.concatenate([hb, ub], axis=1), wcat[1])
            out_f, hf, cf = gate_step(0, sv, b, rf, n, pf, cf, kf)
            out_b, hb, cb = gate_step(1, sv, b, rb, n, pb, cb, kb)
            hc[b, pl.ds(rf, n), 0:H] = out_f
            hc[b, pl.ds(rb, n), H : 2 * H] = out_b
            return hf, hb, cf, cb

        zh, zc = jnp.zeros((n, H), BF16), jnp.zeros((n, H), F32)
        carry = (zh, zh, zc, zc)
        if sec == 1:
            for t in range(steps):
                carry = step(t, carry)
        else:
            lax.fori_loop(0, steps, step, carry, unroll=unroll)

    def norm_forward(b, sec):
        n = 2 * b + sec
        gain, shift = vec[n, 1:2], vec[n, 2:3]

        def fold(body):
            def step(i, acc):
                return acc + jnp.sum(body(pl.multiple_of(i * cr, cr)).reshape(cr // R, R, LANES), axis=0)

            return lax.fori_loop(0, rows // cr, step, jnp.zeros((R, LANES), F32))

        mean = clip_sum(fold(lambda r: valid[pl.ds(r, cr)] * mx[pl.ds(r, cr)])) * inv_count

        def spread(r):
            x = mx[pl.ds(r, cr)].reshape(cr // R, R, LANES) - mean[None]
            return valid[pl.ds(r, cr)] * (x * x).reshape(cr, LANES)

        inv = lax.rsqrt(clip_sum(fold(spread)) * inv_count + 1e-08)
        inv_all[n] = inv

        def apply(r):
            x = (mx[pl.ds(r, cr)].reshape(cr // R, R, LANES) - mean[None]) * inv[None]
            x = x.reshape(cr, LANES)
            normed[n, pl.ds(r, cr)] = x
            stream[pl.ds(r, cr)] += valid[pl.ds(r, cr)] * (x * gain + shift)

        chunks(rows, cr, apply)

    swap = pltpu.make_async_remote_copy(
        src_ref=send, dst_ref=got, send_sem=sems.at[0], recv_sem=sems.at[1], device_id=partner, device_id_type=MESH
    )

    def forward_block(b, carry):
        def u_intra(r):
            u_a[b, pl.ds(r, cr)] = stream[pl.ds(r, cr)].astype(BF16)

        chunks(rows, cr, u_intra)
        run_forward(b, 0, u_a, hc_a, sv_a, R, K, 10)

        @pl.when(b == 0)
        def _():
            pl.semaphore_wait(barrier, len(everyone))
            swap.start()


        mx[0:rows] = dot_nt(hc_a[b], pws[b, 0]) + vec[2 * b, 0:1]
        norm_forward(b, 0)

        run_forward(b, 1, u_e, hc_e, sv_e, kp, R, R)

        xj[...] = dot_nt(hc_e[b], pws[b, 1]) + vec[2 * b + 1, 0:1]
        for k in range(K):
            mx[k * R : (k + 1) * R] = xj[pl.ds(k, R, stride=kp), :]
        norm_forward(b, 1)
        return carry

    lax.fori_loop(0, blocks, forward_block, 0)

    e = enc_ref[...].astype(F32)
    xj[0:frames] = jnp.concatenate([e, e], axis=0).T
    for j in range(R):
        enc_t[pl.ds(j, hop, stride=R), :] = xj[j * hop : (j + 1) * hop]

    first_half = lane < half
    second_half = jnp.logical_and(lane >= half, lane < 2 * half)
    d = dec_in_ref[...].astype(F32)
    d = jnp.concatenate([d, jnp.zeros((LANES - 2 * half, C), F32)], axis=0).T
    dec_ref[0:C, 0:LANES] = jnp.where(first_half, d, 0.0).astype(BF16)
    dec_ref[C : 2 * C, 0:LANES] = jnp.where(second_half, pltpu.roll(d, half, 1), 0.0).astype(BF16)
    dec_ref[0:C, LANES : 2 * LANES] = jnp.where(first_half, pltpu.roll(d, LANES - half, 1), 0.0).astype(BF16)
    dec_ref[C : 2 * C, LANES : 2 * LANES] = jnp.where(second_half, d, 0.0).astype(BF16)

    swap.wait()
    mask_ref[...] = jnp.concatenate([mask_f, got[mask_row : mask_row + C, 0:C]], axis=1).astype(BF16)
    mask_bias = jnp.concatenate(
        [mask_bias_in_ref[0:1].astype(F32), got[mask_row + C : mask_row + C + 1, 0:C]], axis=1
    )
    for q in range(group):
        a = pltpu.roll(own[0:mask_row], LANES - q * half, 1) if q else own[0:mask_row]
        b = pltpu.roll(got[0:mask_row], (LANES - (q - 1) * half) % LANES, 1) if q != 1 else got[0:mask_row]
        w = jnp.where(first_half, a, jnp.where(second_half, b, 0.0))
        xj[pl.ds(q, wr, stride=group), :] = w[0:wr]
    for j in range(R):
        gd[1, j * hop : (j + 1) * hop, 0:LANES] = xj[j * hop : (j + 1) * hop]
    for j in range(R):
        xj[pl.ds(j, hop, stride=R), :] = gd[1, j * hop : (j + 1) * hop, 0:LANES]

    def head_pre(r):
        x = stream[pl.ds(r, cr)]
        f = x * (0.5 * jnp.tanh(0.5 * x) + 0.5)
        f = jnp.where(lane == C, 1.0, f).astype(BF16)
        feats[pl.ds(r, cr)] = f
        pre[pl.ds(r, cr)] = dot(f[:, 0:C], mask_ref[...]) + mask_bias

    chunks(rows, cr, head_pre)

    hr = frames // 5

    def tile(v):
        return jnp.broadcast_to(v[None], (hr // R, R, LANES)).reshape(hr, LANES)

    for q in range(5):
        r = q * hr
        fr = pre[r : r + hr] + tile(not_first) * pre[frames + r - 1 : frames + r - 1 + hr]
        e = enc_t[r : r + hr]
        sp = jnp.maximum(fr, 0.0) + jnp.log1p(jnp.exp(-jnp.abs(fr)))
        masked[r : r + hr] = (sp * e).astype(BF16)
        pre[r : r + hr] = e * (0.5 * jnp.tanh(0.5 * fr) + 0.5)
    for q in range(5):
        r = q * hr
        gd[0, r : r + hr, 0 : 2 * LANES] = dot(masked[r : r + hr], dec_ref[...])
    gd[1, 0:R, 0:LANES] = (
        gd[0, 0:R, 0:LANES] + not_first * gd[0, frames - R - 1 : frames - 1, LANES : 2 * LANES]
    )
    gd[1, R:frames, 0:LANES] = gd[0, R:frames, 0:LANES] + gd[0, 0 : frames - R, LANES : 2 * LANES]
    xj[frames : 2 * frames] = gd[1, 0:frames, 0:LANES]
    for j in range(R):
        gd[1, j * hop : (j + 1) * hop, 0:LANES] = xj[pl.ds(frames + j, hop, stride=R), :]
    xj[frames : 2 * frames] = gd[1, 0:frames, 0:LANES]
    zero = jnp.zeros((wr, LANES), F32)
    w_own, w_far = zero, zero
    for q in range(group):
        x = xj[pl.ds(frames + q, wr, stride=group), :]
        a = jnp.where(first_half, x, 0.0)
        b = jnp.where(second_half, x, 0.0)
        w_own = w_own + (pltpu.roll(a, q * half, 1) if q else a)
        w_far = w_far + (pltpu.roll(b, (q - 1) * half % LANES, 1) if q != 1 else b)
    own[0:wr] = w_own
    send[0:wr] = w_far
    wave_swap = pltpu.make_async_remote_copy(
        src_ref=send.at[0:mask_row],
        dst_ref=wave_got,
        send_sem=sems.at[2],
        recv_sem=sems.at[3],
        device_id=partner,
        device_id_type=MESH,
    )
    wave_swap.start()

    gd[0, 0:frames, 0:LANES] = xj[0:frames]
    gd[0, 0 : frames - R, LANES : 2 * LANES] = xj[R:frames]
    gd[0, frames - R : frames, LANES : 2 * LANES] = next_not_first * xj[1 : R + 1]
    dp[0:frames, 0 : 2 * LANES] = gd[0, 0:frames, 0 : 2 * LANES].astype(BF16)
    g = dot_tn(masked[...], dp[0:frames, 0 : 2 * LANES])
    g_lead = g[0:C, 0:LANES] + pltpu.roll(g[C : 2 * C, 0:LANES], LANES - half, 1)
    g_tail = pltpu.roll(g[0:C, LANES : 2 * LANES], half, 1) + g[C : 2 * C, LANES : 2 * LANES]
    g = jnp.where(first_half, g_lead, g_tail)
    g_dec = jnp.concatenate([g, jnp.zeros_like(g)], axis=0).T[0 : 2 * half]
    xj[frames : frames + 8] = jnp.zeros((8, LANES), F32)
    for q in range(5):
        r = q * hr
        dfr = dot_nt(dp[r : r + hr, 0 : 2 * LANES], dec_ref[...]) * pre[r : r + hr]
        xj[r : r + hr] = dfr
        dpre[r : r + hr] = dfr.astype(BF16)
    for q in range(5):
        r = q * hr
        dpre[frames + r : frames + r + hr] = (tile(next_not_first) * xj[r + 1 : r + 1 + hr]).astype(BF16)
    gm = dot_tn(feats[...], dpre[...])
    gm = jnp.where(speaker == 0, gm, pltpu.roll(gm, C, 1))
    n, at = 2 * blocks - 1, lay["head"]
    for q in range(4):
        sums[n, at : at + 16, q * LANES : (q + 1) * LANES] = gm[16 * q : 16 * q + 16].astype(BF16)
    sums[n, at + 16 : at + 32, 0:LANES] = jnp.where(lane < C, g_dec, 0.0).astype(BF16)
    sums[n, at + 16 : at + 32, LANES : 2 * LANES] = jnp.broadcast_to(gm[C : C + 1], (16, LANES)).astype(BF16)
    dz[...] = jnp.zeros_like(dz)

    def head_dz(r):
        x = stream[pl.ds(r, cr)]
        sg = 0.5 * jnp.tanh(0.5 * x) + 0.5
        df = dot_nt(dpre[pl.ds(r, cr)], mask_ref[...])
        df = jnp.concatenate([df, jnp.zeros_like(df)], axis=1)
        dz[pl.ds(r, cr)] = df * sg * (1.0 + x * (1.0 - sg))

    chunks(rows, cr, head_dz)

    def norm_backward(b, sec):
        n = 2 * b + sec
        gain = vec[n, 1:2]

        def sums(i, acc):
            r = pl.multiple_of(i * cr, cr)
            v = valid[pl.ds(r, cr)] * dz[pl.ds(r, cr)]
            w = v * normed[n, pl.ds(r, cr)]
            return (
                acc[0] + jnp.sum(v.reshape(cr // R, R, LANES), axis=0),
                acc[1] + jnp.sum(w.reshape(cr // R, R, LANES), axis=0),
            )

        zero = jnp.zeros((R, LANES), F32)
        s1, s2 = lax.fori_loop(0, rows // cr, sums, (zero, zero))
        small[1:2, LANES : 2 * LANES] = jnp.sum(s2, axis=0, keepdims=True)
        small[1:2, 2 * LANES : 3 * LANES] = jnp.sum(s1, axis=0, keepdims=True)
        m1 = clip_sum(s1 * gain) * inv_count
        m2 = clip_sum(s2 * gain) * inv_count
        inv = inv_all[n]

        def apply(i, acc):
            r = pl.multiple_of(i * cr, cr)
            d = (dz[pl.ds(r, cr)] * gain).reshape(cr // R, R, LANES)
            x = normed[n, pl.ds(r, cr)].reshape(cr // R, R, LANES)
            y = (d - m1[None] - x * m2[None]) * inv[None]
            y = (y.reshape(cr, LANES) * valid[pl.ds(r, cr)]).astype(BF16)
            if sec == 0:
                dmj[pl.ds(r, cr)] = y
            y = y.astype(F32)
            if sec == 1:
                mx[pl.ds(r, cr)] = y
            return acc + jnp.sum(y.reshape(cr // R, R, LANES), axis=0)

        acc = lax.fori_loop(0, rows // cr, apply, zero)
        small[1:2, 0:LANES] = jnp.sum(acc, axis=0, keepdims=True)

    def back_step(d, sv, b, r, n, dhn, dcn, keep):
        a = [sv[b, d, pl.ds(r, n), m * H : (m + 1) * H].astype(F32) for m in range(6)]
        g = dh[pl.ds(r, n), d * H : (d + 1) * H] + dhn
        dc = dcn + g * a[4]
        for m in range(4):
            dp[pl.ds(r, n), (4 * d + m) * H : (4 * d + m + 1) * H] = ((g if m == 3 else dc) * a[m]).astype(BF16)
        dhn = dot(dp[pl.ds(r, n), 4 * d * H : 4 * (d + 1) * H], wrt[d])
        dcn = dc * a[5]
        if keep is not None:
            dhn, dcn = dhn * keep, dcn * keep
        return dhn, dcn

    def run_backward(b, sec, u, hc, sv, n, steps, unroll, parts):
        total = n * steps
        out = sums.at[2 * b + sec]
        g = dot_tn(dmj[0:total], hc[b])[0:C].astype(BF16)
        at = lay["proj"]
        out[at : at + C // 2, 0 : 2 * H] = g[0 : C // 2]
        out[at : at + C // 2, 2 * H : 4 * H] = g[C // 2 : C]

        dh[0:total] = dot(dmj[0:total], pws[b, sec])
        for d in range(2):
            wrt[d] = w_rec_ref[b, sec, d].T
            wit[d * 4 * H : (d + 1) * 4 * H, 0:C] = w_in_ref[b, sec, d].T

        def step(t, carry):
            hf, hb, cf, cb = carry
            back = steps - 1 - t
            rf = pl.multiple_of(back * n, n)
            rb = pl.multiple_of(t * n, n)
            kf = kb = None
            if sec == 1:
                kf = 1.0 - is_start(back).astype(F32)
                kb = 1.0 - is_end(t).astype(F32)
            hf, cf = back_step(0, sv, b, rf, n, hf, cf, kf)
            hb, cb = back_step(1, sv, b, rb, n, hb, cb, kb)
            return hf, hb, cf, cb

        z = jnp.zeros((n, H), F32)
        carry = (z, z, z, z)
        point(2.5)
        for p in range(parts):
            carry = lax.fori_loop(p * steps // parts, (p + 1) * steps // parts, step, carry, unroll=unroll)
            point(steps * 0.125 / parts)
        if sec == 1:
            for j in range(1, steps):
                kf = (1.0 - is_start(j).astype(F32)).astype(BF16)
                at = slice((j - 1) * n, j * n)
                hc[b, at, 0:H] = hc[b, at, 0:H] * kf
                kb = (1.0 - is_end(j - 1).astype(F32)).astype(BF16)
                at = slice(j * n, (j + 1) * n)
                hc[b, at, H : 2 * H] = hc[b, at, H : 2 * H] * kb
        last = (b, sec) == (0, 0)
        core = place.bit(0)
        reduce = reduction(2 * b + sec, [[0], near + far] if b == 0 else [[0], near, far])
        for d in (1 - core, core):
            gates = pl.ds(pl.multiple_of(4 * d * H, H), 4 * H)
            g = dot_tn(u[b], dp[0:total, gates])
            base = d * lay["half"]
            out[pl.ds(pl.multiple_of(base + lay["in"], PART), C)] = g[0:C].astype(BF16)
            small[0:1] = g[C : C + 1]
            out[pl.ds(pl.multiple_of(base + lay["small"], PART), 16)] = small[...].astype(BF16)
            h_prev = hc[b, pl.ds(pl.multiple_of(d * n, n), total - n), pl.ds(pl.multiple_of(d * H, H), H)]
            g = dot_tn(h_prev, dp[pl.ds(pl.multiple_of((1 - d) * n, n), total - n), gates])
            out[pl.ds(pl.multiple_of(base + lay["rec"], PART), H)] = g.astype(BF16)
            if d is core:
                point(0.6)
            else:
                reduce.advance(clock[0] + 0.6)
                active.append(reduce)

    def stream_grad(total):
        return dot(dp[0:total], wit[...])

    small[...] = jnp.zeros_like(small)
    for b in reversed(range(blocks)):
        norm_backward(b, 1)
        mx[rows:rows_e] = jnp.zeros((rows_e - rows, LANES), F32)
        for j in range(R):
            dmj[pl.ds(j * kp, kp)] = mx[pl.ds(j, kp, stride=R), :].astype(BF16)
        run_backward(b, 1, u_e, hc_e, sv_e, kp, R, R, 1)

        xj[...] = stream_grad(rows_e)
        for k in range(K):
            dz[k * R : (k + 1) * R] += xj[pl.ds(k, R, stride=kp), :]
        point(1.5)

        norm_backward(b, 0)
        run_backward(b, 0, u_a, hc_a, sv_a, R, K, 10, 5)

        dz[0:rows] += stream_grad(rows)
        point(1.5)

    def finish(r):
        dz[pl.ds(r, cr)] = dz[pl.ds(r, cr)] * valid[pl.ds(r, cr)]

    chunks(rows, cr, finish)
    for j in range(R):
        grad_spans[j] = dz[pl.ds(j, K, stride=R), :].T[0:C]
    exits = [pltpu.make_async_copy(grad_spans, spans_out, out_sems.at[2 * blocks])]
    exits[0].start()
    wave_swap.wait()
    for i in range(wr):
        at = pl.multiple_of(speaker * (wr * LANES) + i * LANES, LANES)
        wave_out[0:1, pl.ds(at, LANES)] = own[i : i + 1]
        at = pl.multiple_of((1 - speaker) * (wr * LANES) + i * LANES, LANES)
        wave_out[0:1, pl.ds(at, LANES)] = wave_got[i : i + 1]

    left = list(active)
    while left:
        for reduce in [reduce for reduce in left if reduce.over()]:
            n = reduce.number
            exits.append(pltpu.make_async_copy(all_sums.at[n], sums_out.at[n], out_sems.at[n]))
            exits[-1].start()
            left.remove(reduce)
        if left:
            nearest = min(left, key=lambda reduce: reduce.due)
            clock[0] = max(clock[0], nearest.due)
            nearest.advance(clock[0])
    for copy in exits:
        copy.wait()


def unpack_kernel(
    sizes,
    sums,
    wave_in,
    spans_in,
    wave_out,
    spans_out,
    in_out,
    rec_out,
    bias_out,
    proj_out,
    proj_bias_out,
    gain_out,
    shift_out,
    mask_out,
    mask_bias_out,
    dec_out,
):
    C, H = sizes
    lay = sum_rows(C, H)
    n = pl.program_id(0)
    b, sec = n // 2, n % 2
    speaker = lax.axis_index("spk")
    spans_out[...] = spans_in[...]
    for d in range(2):
        base = d * lay["half"]
        in_out[d] = sums[base + lay["in"] : base + lay["in"] + C].astype(F32)
        rec_out[d] = sums[base + lay["rec"] : base + lay["rec"] + H].astype(F32)
        small = sums[base + lay["small"] : base + lay["small"] + 16].astype(F32)
        bias_out[d : d + 1] = small[0:1]
        if d == 0:
            for m, out in enumerate((proj_bias_out, gain_out, shift_out)):
                out[b, pl.ds(sec, 1)] = small[1:2, m * LANES : m * LANES + C]
    at = lay["proj"]
    proj_out[0 : C // 2] = sums[at : at + C // 2, 0 : 2 * H].astype(F32)
    proj_out[C // 2 : C] = sums[at : at + C // 2, 2 * H : 4 * H].astype(F32)

    @pl.when(n == 0)
    def _():
        wave_out[...] = wave_in[...]

    @pl.when(n == pl.num_programs(0) - 1)
    def _():
        at = lay["head"]

        def own(x):
            return jnp.where(speaker == 0, x, pltpu.roll(x, C, 1))[:, 0:C]

        for q in range(4):
            x = sums[at : at + 16, q * LANES : (q + 1) * LANES].astype(F32)
            mask_out[0, 16 * q : 16 * q + 16] = own(x)
        x = sums[at + 16 : at + 32, 0 : 2 * LANES].astype(F32)
        mask_bias_out[...] = own(x[:, LANES : 2 * LANES])[0:1]
        dec_out[...] = x[:, 0:C]


def sum_rows(C, H):
    lay, at = {}, 0
    for name, rows in (("in", C), ("rec", H), ("small", 16), ("proj", C // 2)):
        lay[name] = at
        at += rows
    lay["half"] = -(-at // (16 * PART)) * 16 * PART
    lay["head"] = lay["half"] + lay["proj"]
    lay["total"] = 2 * lay["half"]
    return lay


def shards(
    num_dp,
    spans,
    encoded,
    clip_lengths,
    clip_pads,
    lstm_in,
    lstm_rec,
    lstm_bias,
    proj_weight,
    proj_bias,
    gln_gain,
    gln_shift,
    mask_weight,
    mask_bias,
    dec_weight,
    wave_grad,
):
    R, K, C = spans.shape
    H = lstm_rec.shape[3]
    blocks = lstm_in.shape[0]
    clips = clip_lengths.shape[2]
    frames = encoded.shape[0]
    half = dec_weight.shape[1] // 2
    kp = -(-K // 16) * 16
    rows, rows_e = R * K, R * kp
    wr = frames * half // LANES
    mask_row = -(-wr // 8) * 8

    sizes = (R, K, C, H, clips, blocks, kp, num_dp)
    lay = sum_rows(C, H)
    outer = max(num_dp.bit_length() - 5, 0)
    smem = pl.BlockSpec(memory_space=pltpu.SMEM)
    vmem = pl.BlockSpec(memory_space=pltpu.VMEM)
    shape = jax.ShapeDtypeStruct
    outs = pl.pallas_call(
        functools.partial(local_kernel, sizes),
        out_shape=(
            shape((1, 2 * frames * half), F32),
            shape((R, C, K), F32),
            shape((2 * blocks, lay["total"], 4 * H), BF16),
        ),
        in_specs=[smem, smem] + [vmem] * 13,
        out_specs=(vmem, pl.BlockSpec(memory_space=pl.ANY), pl.BlockSpec(memory_space=pl.ANY)),
        scratch_shapes=[
            pltpu.VMEM((rows_e, LANES), F32),
            pltpu.VMEM((rows, LANES), F32),
            pltpu.VMEM((rows_e, LANES), F32),
            pltpu.VMEM((rows_e, LANES), F32),
            pltpu.VMEM((rows_e, LANES), F32),
            pltpu.VMEM((rows_e, LANES), BF16),
            pltpu.VMEM((2 * blocks, rows, LANES), F32),
            pltpu.VMEM((2 * blocks, R, LANES), F32),
            pltpu.VMEM((blocks, rows, LANES), BF16),
            pltpu.VMEM((blocks, rows_e, LANES), BF16),
            pltpu.VMEM((blocks, rows, 2 * H), BF16),
            pltpu.VMEM((blocks, rows_e, 2 * H), BF16),
            pltpu.VMEM((blocks, 2, rows, 6 * H), BF16),
            pltpu.VMEM((blocks, 2, rows_e, 6 * H), BF16),
            pltpu.VMEM((2, frames, 2 * LANES), F32),
            pltpu.VMEM((rows_e, 2 * H), F32),
            pltpu.VMEM((rows_e, 8 * H), BF16),
            pltpu.VMEM((2, 2 * H, 4 * H), BF16),
            pltpu.VMEM((8 * H, LANES), BF16),
            pltpu.VMEM((2, 4 * H, H), BF16),
            pltpu.VMEM((blocks, 2, LANES, 2 * H), BF16),
            pltpu.VMEM((2 * blocks, 8, LANES), F32),
            pltpu.VMEM((frames, LANES), F32),
            pltpu.VMEM((rows, LANES), F32),
            pltpu.VMEM((frames, LANES), BF16),
            pltpu.VMEM((rows, LANES), BF16),
            pltpu.VMEM((rows, LANES), BF16),
            pltpu.VMEM((C, 2 * C), BF16),
            pltpu.VMEM((2 * C, 2 * LANES), BF16),
            pltpu.VMEM((mask_row + C + 8, LANES), F32),
            pltpu.VMEM((mask_row, LANES), F32),
            pltpu.VMEM((mask_row + C + 8, LANES), F32),
            pltpu.VMEM((mask_row, LANES), F32),
            pltpu.SemaphoreType.DMA((4,)),
            pltpu.VMEM((2 * blocks, lay["total"], 4 * H), BF16),
            pltpu.VMEM((2 * blocks, lay["total"] + PART * outer, 4 * H), BF16),
            pltpu.VMEM((16, 4 * H), F32),
            pltpu.SemaphoreType.DMA((2 * blocks, 6 + outer, 2)),
            pltpu.VMEM((2 * blocks, lay["total"], 4 * H), BF16),
            pltpu.VMEM((R, C, K), F32),
            pltpu.SemaphoreType.DMA((2 * blocks + 1,)),
        ],
        compiler_params=pltpu.CompilerParams(
            vmem_limit_bytes=62 * 1024 * 1024, collective_id=0, has_side_effects=True
        ),
        name="dual_path",
    )(
        clip_lengths,
        clip_pads,
        spans.transpose(0, 2, 1),
        encoded.T,
        lstm_in,
        lstm_rec,
        lstm_bias,
        proj_weight.transpose(0, 1, 3, 2),
        proj_bias,
        gln_gain,
        gln_shift,
        mask_weight,
        mask_bias,
        dec_weight.T,
        wave_grad,
    )
    half = dec_weight.shape[1] // 2
    per_section = pl.BlockSpec((None, lay["total"], 4 * H), lambda n: (n, 0, 0))

    def whole(*dims):
        return pl.BlockSpec(dims, lambda n: (0,) * len(dims))

    def section(*dims):
        return pl.BlockSpec((None, None) + dims, lambda n: (n // 2, n % 2) + (0,) * len(dims))

    finals = pl.pallas_call(
        functools.partial(unpack_kernel, (C, H)),
        grid=(2 * blocks,),
        out_shape=(
            shape((1, 2 * frames * half), F32),
            shape((R, C, K), F32),
            shape((blocks, 2, 2, C, 4 * H), F32),
            shape((blocks, 2, 2, H, 4 * H), F32),
            shape((blocks, 2, 2, 4 * H), F32),
            shape((blocks, 2, C, 2 * H), F32),
            shape((blocks, 2, C), F32),
            shape((blocks, 2, C), F32),
            shape((blocks, 2, C), F32),
            shape((1, C, C), F32),
            shape((1, C), F32),
            shape((2 * half, C), F32),
        ),
        in_specs=[
            per_section,
            whole(1, 2 * frames * half),
            pl.BlockSpec((R // (2 * blocks), C, K), lambda n: (n, 0, 0)),
        ],
        out_specs=(
            whole(1, 2 * frames * half),
            pl.BlockSpec((R // (2 * blocks), C, K), lambda n: (n, 0, 0)),
            section(2, C, 4 * H),
            section(2, H, 4 * H),
            section(2, 4 * H),
            section(C, 2 * H),
            whole(blocks, 2, C),
            whole(blocks, 2, C),
            whole(blocks, 2, C),
            whole(1, C, C),
            whole(1, C),
            whole(2 * half, C),
        ),
        compiler_params=pltpu.CompilerParams(vmem_limit_bytes=60 * 1024 * 1024),
        name="unpack",
    )(outs[2], outs[0], outs[1])
    return (
        finals[0],
        finals[1].transpose(0, 2, 1),
        finals[2],
        finals[3],
        finals[4],
        finals[5].transpose(0, 1, 3, 2),
        finals[6],
        finals[7],
        finals[8],
        finals[9],
        finals[10],
        finals[11].T,
    )


def solution(mesh):
    return jax.shard_map(
        functools.partial(shards, mesh.shape["dp"]),
        mesh=mesh,
        in_specs=(
            P(("dp", "spk"), None, None),
            P(("dp", "spk"), None),
            P("dp", None, None),
            P("dp", None, None),
            P(),
            P(),
            P(),
            P(),
            P(),
            P(),
            P(),
            P("spk", None, None),
            P("spk", None),
            P(),
            P("spk", "dp"),
        ),
        out_specs=(
            P("spk", "dp"),
            P(("dp", "spk"), None, None),
            P(),
            P(),
            P(),
            P(),
            P(),
            P(),
            P(),
            P("spk", None, None),
            P("spk", None),
            P(),
        ),
        check_vma=False,
    )
```

profile of v0, /device:TPU:0, one launch (start us, length us, event | category | flops | bytes accessed | tf_op | source)
XLA Modules:
  0.0 123.0 jit_solution(3190048443557545631)
XLA Ops:
  0.7 117.7 %dual_path.1 = (f32[1,12800]{1,0:T(1,128)}, f32[16,64,100]{2,1,0:T(8,128)}, bf16[4,512,512]{2,1,0:T(8,128)(2,1)}) custom-call(s32[1,2,3]{2,1,0:T(2,128)} %lengths_ref.1, s32[1,2,3]{2,1,0:T(2,128)} %pads_ref.1, bf16[16,64,100]{2,1,0:T(8,128)(2,1)} %bitcast.7, bf16[64,800]{1,0:T(8,128)(2,1)} %bitcast.9, bf16[2,2,2,64,512]{4,3,2,1,0:T(8,128)(2,1)} %w_in_ref.1, ...), custom_call_target="tpu_custom_call" | custom-call | tf_op jit(solution)/shard_map/dual_path/pallas_call | solution.py:876
  118.4 4.4 %unpack.1 = (f32[1,12800]{1,0:T(1,128)}, f32[16,64,100]{2,1,0:T(8,128)}, f32[2,2,2,64,512]{4,3,2,1,0:T(8,128)}, f32[2,2,2,128,512]{4,3,2,1,0:T(8,128)}, f32[2,2,...) custom-call(bf16[4,512,512]{2,1,0:T(8,128)(2,1)} %get-tuple-element., ...), custom_call_target="tpu_custom_call" | custom-call | tf_op jit(solution)/shard_map/unpack/pallas_call | solution.py:958
where the time goes:
time: 123 us
  Pallas kernels  122 us (99%)
    pallas_call x1, Pallas kernels, shards(): pl.pallas_call(functools.partial(local_kernel, sizes), out_shape=(shape((...  118 us
    pallas_call x1, Pallas kernels, shards(): pl.pallas_call(functools.partial(unpack_kernel, (C, H)), grid=(2 * blocks...  4.37 us

commit v1 on v0

--- a/solution.py
+++ b/solution.py
@@ -316,7 +316,7 @@
 
     near, far = list(range(1, min(place.bits, 3))), list(range(3, min(place.bits, 5)))
     outer = range(5, place.bits)
-    times = {1: 1.7, 2: 4.2, 4: 6.8}
+    times = {1: 2.2, 2: 5.0, 4: 8.0}
 
     def reduction(n, stages):
         reduce = Reduction(sums.at[n], recv.at[n], all_sums.at[n], sum_sems.at[n], place, stages, outer, times)

time: 123 us -> 122 us (level)
  no operation moved by 1% of the time
where the time goes in v1:
time: 122 us
  Pallas kernels  121 us (99%)
    pallas_call x1, Pallas kernels, shards(): pl.pallas_call(functools.partial(local_kernel, sizes), out_shape=(shape((...  117 us
    pallas_call x1, Pallas kernels, shards(): pl.pallas_call(functools.partial(unpack_kernel, (C, H)), grid=(2 * blocks...  4.37 us

profile of v1, /device:TPU:0, one launch (start us, length us, event | category | flops | bytes accessed | tf_op | source)
XLA Modules:
  0.0 121.9 jit_solution(11224950002920370273)
XLA Ops:
  0.7 116.7 %dual_path.1 = (f32[1,12800]{1,0:T(1,128)}, f32[16,64,100]{2,1,0:T(8,128)}, bf16[4,512,512]{2,1,0:T(8,128)(2,1)}) custom-call(s32[1,2,3]{2,1,0:T(2,128)} %lengths_ref.1, s32[1,2,3]{2,1,0:T(2,128)} %pads_ref.1, bf16[16,64,100]{2,1,0:T(8,128)(2,1)} %bitcast.7, bf16[64,800]{1,0:T(8,128)(2,1)} %bitcast.9, bf16[2,2,2,64,512]{4,3,2,1,0:T(8,128)(2,1)} %w_in_ref.1, ...), custom_call_target="tpu_custom_call" | custom-call | tf_op jit(solution)/shard_map/dual_path/pallas_call | solution.py:876
  117.4 4.4 %unpack.1 = (f32[1,12800]{1,0:T(1,128)}, f32[16,64,100]{2,1,0:T(8,128)}, f32[2,2,2,64,512]{4,3,2,1,0:T(8,128)}, f32[2,2,2,128,512]{4,3,2,1,0:T(8,128)}, f32[2,2,...) custom-call(bf16[4,512,512]{2,1,0:T(8,128)(2,1)} %get-tuple-element., ...), custom_call_target="tpu_custom_call" | custom-call | tf_op jit(solution)/shard_map/unpack/pallas_call | solution.py:958
